TPU v7x, 256 devices: a whole 4x4x8 slice. The times are simulated.
256 devices in a mesh: pipe: 4 (over z_lo, core), fsdp: 64 (over x, z_hi, y).
Axes of the slice: x: 4, y: 4, z: 8 (z_hi: 4, z_lo: 2; z = z_hi * 2 + z_lo), core: 2. Of those that a mesh axis runs over, the one named last changes fastest.
Arguments:
- tokens: int32 [2, 160], replicated, may hold values from 0 to 511
- embed: bfloat16 [512, 8192], P(None, 'fsdp'), may hold values from -60 to 60
- gain: bfloat16 [4, 8192], P('pipe', 'fsdp'), may hold values from 0.099609375 to 1.8984375
- w_in: bfloat16 [4, 3, 8192, 8192], P('pipe', None, None, 'fsdp'), may hold values from -0.0625 to 0.0625
- short_filter: float32 [4, 3, 7, 8192], P('pipe', None, None, 'fsdp'), may hold values from -2 to 2
- long_filter: float32 [4, 512, 128], P('pipe', 'fsdp'), may hold values from -0.5 to 0.5
- skip_bias: float32 [4, 8192], P('pipe', 'fsdp'), may hold values from -1 to 1
- w_out: bfloat16 [4, 8192, 8192], P('pipe', None, 'fsdp'), may hold values from -0.0625 to 0.0625
Outputs:
- hidden: bfloat16 [2, 160, 8192], P(None, 'pipe', 'fsdp')
All inputs are finite; a program needn't handle non-finite values.
Results may differ from a plain program's by a relative error of at most 0.035.
Values may be sent and summed in bfloat16 or wider, within the bound.
No kernel may reach another device: no remote copies, remote signals or barrier semaphores. Data moves between devices by JAX's collectives and lax.ppermute only.
A program may use at most 64 MiB of HBM per device.

v0:
```python
import jax
import jax.numpy as jnp
from jax import lax
from jax.sharding import PartitionSpec as P

D = 8192
GROUP = 16


def from_behind(block, axis, distance):
    devices = range(lax.axis_size(axis))
    route = [(i - distance, i) for i in devices if i - distance in devices]
    return lax.ppermute(block, axis, route)


def spread(value, axis, root):
    mine = lax.axis_index(axis) == root
    return lax.psum(jnp.where(mine, value, jnp.zeros_like(value)), axis)


def short_mix(projected, filters):
    width = filters.shape[1]
    seq_len = projected.shape[1]
    padded = jnp.pad(projected.astype(jnp.float32), ((0, 0), (width - 1, 0), (0, 0)))
    running = jnp.zeros(projected.shape, jnp.float32)
    for offset in range(width):
        window = padded[:, width - 1 - offset : width - 1 - offset + seq_len, :]
        running = running + filters[:, offset][:, None, :] * window
    return running


def long_mix(signal, kernels, group_size):
    seq_len = signal.shape[0]
    span = kernels.shape[1]
    count_filters = kernels.shape[0]
    positions = jnp.arange(seq_len, dtype=jnp.int32)
    lag_table = positions[:, None] - positions[None, :]
    inside = (lag_table >= 0) & (lag_table < span)
    lag_index = jnp.clip(lag_table, 0, span - 1)
    toeplitz = jnp.where(inside[None, :, :], kernels[:, lag_index], jnp.float32(0.0))
    grouped = signal.reshape(seq_len, count_filters, group_size)
    mixed = jnp.einsum("fts,sfg->tfg", toeplitz, grouped, precision=lax.Precision.HIGHEST)
    return mixed.reshape(seq_len, count_filters * group_size)


def body(tokens, embed, gain, w_in, short_filter, long_filter, skip_bias, w_out):
    segment_count = lax.axis_size("pipe")
    segment_index = lax.axis_index("pipe")
    batch_count = tokens.shape[0]
    seq_len = tokens.shape[1]
    local_width = embed.shape[1]
    in_weights = w_in[0]
    short_taps = short_filter[0]
    long_taps = long_filter[0]
    skip_row = skip_bias[0]
    out_weight = w_out[0]
    vocab_index = jnp.arange(embed.shape[0], dtype=jnp.int32)

    def layer_step(activation):
        widened = activation.astype(jnp.float32)
        squares = lax.psum(jnp.sum(widened * widened, axis=1), "fsdp")
        inverse_rms = lax.rsqrt(squares / D + 1e-06)[:, None]
        normalized = (widened * inverse_rms * gain.astype(jnp.float32)).astype(jnp.bfloat16)
        weight_rows = in_weights
        projected = jnp.einsum(
            "sk,jkc->jsc",
            lax.all_gather(normalized, "fsdp", axis=1, tiled=True),
            weight_rows,
            preferred_element_type=jnp.float32,
        )
        mixed = short_mix(projected.astype(jnp.bfloat16), short_taps)
        product = mixed[1] * mixed[2]
        carried = long_mix(product, long_taps, GROUP) + skip_row[None, :] * product
        gated = (mixed[0] * carried).astype(jnp.bfloat16)
        weight_rows = out_weight
        projected_out = jnp.dot(
            lax.all_gather(gated, "fsdp", axis=1, tiled=True),
            weight_rows,
            preferred_element_type=jnp.float32,
        )
        return (widened + projected_out).astype(jnp.bfloat16)

    def tick_body(tick_index, carry_state):
        previous, collected = carry_state
        incoming = from_behind(previous, "pipe", 1)
        micro_index = tick_index - segment_index
        chosen = jnp.clip(micro_index, 0, batch_count - 1)
        token_ids = lax.dynamic_index_in_dim(tokens, chosen, 0, keepdims=False)
        one_hot = (token_ids[:, None] == vocab_index[None, :]).astype(jnp.bfloat16)
        embedded = jnp.dot(one_hot, embed, preferred_element_type=jnp.float32).astype(jnp.bfloat16)
        activation = jnp.where(segment_index == 0, embedded, incoming)
        layer_out = layer_step(activation)
        store_flag = (
            (micro_index >= 0) & (micro_index < batch_count) & (segment_index == segment_count - 1)
        )
        updated = lax.dynamic_update_index_in_dim(collected, layer_out, chosen, 0)
        collected = jnp.where(store_flag, updated, collected)
        return (layer_out, collected)

    start_state = (
        jnp.zeros((seq_len, local_width), jnp.bfloat16),
        jnp.zeros((batch_count, seq_len, local_width), jnp.bfloat16),
    )
    final_state = lax.fori_loop(0, batch_count + segment_count - 1, tick_body, start_state)
    finished = spread(final_state[1], "pipe", segment_count - 1)
    row_share = seq_len // segment_count
    return lax.dynamic_slice_in_dim(finished, segment_index * row_share, row_share, 1)


def solution(mesh):
    return jax.shard_map(
        body,
        mesh=mesh,
        in_specs=(
            P(),
            P(None, "fsdp"),
            P("pipe", "fsdp"),
            P("pipe", None, None, "fsdp"),
            P("pipe", None, None, "fsdp"),
            P("pipe", "fsdp", None),
            P("pipe", "fsdp"),
            P("pipe", None, "fsdp"),
        ),
        out_specs=P(None, "pipe", "fsdp"),
        check_vma=False,
    )
```

profile of v0, /device:TPU:1, one launch (start us, length us, event | category | flops | bytes accessed | tf_op | source)
XLA Modules:
  0.0 2043.1 jit_solution(8263287136697875596)
XLA Ops:
  10.1 1982.0 %while.18 = (s32[]{:T(128)}, bf16[160,128]{1,0:T(8,128)(2,1)}, bf16[2,160,128]{2,1,0:T(8,128)(2,1)}, pred[]{:T(512)}, s32[]{:T(128)}, /*index=5*/s32[2,160]{1,0:...) while((s32[]{:T(128)}, bf16[160,128]{1,0:T(8,128)(2,1)}, ...), condition=%wide.region_3.4_spmd.clone, body=%wide.region_0.3_spmd.clone.sunk | while | flops 1404303872 | bytes 46493152 | solution.py:104
  17.7 168.4 %psum.24 = f32[160]{0:T(256)S(1)} all-reduce(f32[160]{0:T(256)S(1)} %get-tuple-element.508), channel_id=1, replica_groups=mesh['pipe'=4,'fsdp'=64] {'fsdp'}, use_global_device_ids=true, to_apply=%region_2.2 | all-reduce | flops 160 | bytes 1280 | tf_op jit(solution)/shard_map/while/body/eval_jaxpr/psum | solution.py:61
  187.1 85.3 %gather_fusion = f32[25600,8]{1,0:T(8,128)} fusion(f32[8,128]{0,1:T(8,128)S(1)} %get-tuple-element.562, s32[25600]{0:T(1024)S(1)} %broadcast_clamp_fusion.2), kind=kCustom, calls=%fused_computation.clone.clone.1 | custom fusion | bytes 1740800 | tf_op jit(solution)/shard_map/while/body/eval_jaxpr/gather | solution.py:40
  283.2 13.5 all-gather.3.cloned.1.call-done
  310.4 96.4 %all-gather.5.cloned.1.call-done = bf16[160,8192]{1,0:T(8,128)(2,1)} async-done(((bf16[160,128]{1,0:T(8,128)(2,1)}), bf16[160,8192]{1,0:T(8,128)(2,1)}) %all-gather.5.cloned.1.call-update) | async-done | bytes 2621456 | tf_op jit(solution)/shard_map/while/body/eval_jaxpr/all_gather | solution.py:77
  415.4 166.0 %psum.24 = f32[160]{0:T(256)S(1)} all-reduce(f32[160]{0:T(256)S(1)} %get-tuple-element.508), channel_id=1, replica_groups=mesh['pipe'=4,'fsdp'=64] {'fsdp'}, use_global_device_ids=true, to_apply=%region_2.2 | all-reduce | flops 160 | bytes 1280 | tf_op jit(solution)/shard_map/while/body/eval_jaxpr/psum | solution.py:61
  582.4 85.3 %gather_fusion = f32[25600,8]{1,0:T(8,128)} fusion(f32[8,128]{0,1:T(8,128)S(1)} %get-tuple-element.562, s32[25600]{0:T(1024)S(1)} %broadcast_clamp_fusion.2), kind=kCustom, calls=%fused_computation.clone.clone.1 | custom fusion | bytes 1740800 | tf_op jit(solution)/shard_map/while/body/eval_jaxpr/gather | solution.py:40
  678.5 13.8 all-gather.3.cloned.1.call-done
  706.1 96.3 %all-gather.5.cloned.1.call-done = bf16[160,8192]{1,0:T(8,128)(2,1)} async-done(((bf16[160,128]{1,0:T(8,128)(2,1)}), bf16[160,8192]{1,0:T(8,128)(2,1)}) %all-gather.5.cloned.1.call-update) | async-done | bytes 2621456 | tf_op jit(solution)/shard_map/while/body/eval_jaxpr/all_gather | solution.py:77
  810.9 166.0 %psum.24 = f32[160]{0:T(256)S(1)} all-reduce(f32[160]{0:T(256)S(1)} %get-tuple-element.508), channel_id=1, replica_groups=mesh['pipe'=4,'fsdp'=64] {'fsdp'}, use_global_device_ids=true, to_apply=%region_2.2 | all-reduce | flops 160 | bytes 1280 | tf_op jit(solution)/shard_map/while/body/eval_jaxpr/psum | solution.py:61
  977.9 85.3 %gather_fusion = f32[25600,8]{1,0:T(8,128)} fusion(f32[8,128]{0,1:T(8,128)S(1)} %get-tuple-element.562, s32[25600]{0:T(1024)S(1)} %broadcast_clamp_fusion.2), kind=kCustom, calls=%fused_computation.clone.clone.1 | custom fusion | bytes 1740800 | tf_op jit(solution)/shard_map/while/body/eval_jaxpr/gather | solution.py:40
  1063.1 8.8 copy.25
  1074.0 13.8 all-gather.3.cloned.1.call-done
  1101.6 96.3 %all-gather.5.cloned.1.call-done = bf16[160,8192]{1,0:T(8,128)(2,1)} async-done(((bf16[160,128]{1,0:T(8,128)(2,1)}), bf16[160,8192]{1,0:T(8,128)(2,1)}) %all-gather.5.cloned.1.call-update) | async-done | bytes 2621456 | tf_op jit(solution)/shard_map/while/body/eval_jaxpr/all_gather | solution.py:77
  1206.4 166.0 %psum.24 = f32[160]{0:T(256)S(1)} all-reduce(f32[160]{0:T(256)S(1)} %get-tuple-element.508), channel_id=1, replica_groups=mesh['pipe'=4,'fsdp'=64] {'fsdp'}, use_global_device_ids=true, to_apply=%region_2.2 | all-reduce | flops 160 | bytes 1280 | tf_op jit(solution)/shard_map/while/body/eval_jaxpr/psum | solution.py:61
  1373.4 85.3 %gather_fusion = f32[25600,8]{1,0:T(8,128)} fusion(f32[8,128]{0,1:T(8,128)S(1)} %get-tuple-element.562, s32[25600]{0:T(1024)S(1)} %broadcast_clamp_fusion.2), kind=kCustom, calls=%fused_computation.clone.clone.1 | custom fusion | bytes 1740800 | tf_op jit(solution)/shard_map/while/body/eval_jaxpr/gather | solution.py:40
  1458.6 8.8 copy.25
  1469.5 13.8 all-gather.3.cloned.1.call-done
  1497.1 96.3 %all-gather.5.cloned.1.call-done = bf16[160,8192]{1,0:T(8,128)(2,1)} async-done(((bf16[160,128]{1,0:T(8,128)(2,1)}), bf16[160,8192]{1,0:T(8,128)(2,1)}) %all-gather.5.cloned.1.call-update) | async-done | bytes 2621456 | tf_op jit(solution)/shard_map/while/body/eval_jaxpr/all_gather | solution.py:77
  1601.9 166.0 %psum.24 = f32[160]{0:T(256)S(1)} all-reduce(f32[160]{0:T(256)S(1)} %get-tuple-element.508), channel_id=1, replica_groups=mesh['pipe'=4,'fsdp'=64] {'fsdp'}, use_global_device_ids=true, to_apply=%region_2.2 | all-reduce | flops 160 | bytes 1280 | tf_op jit(solution)/shard_map/while/body/eval_jaxpr/psum | solution.py:61
  1768.9 85.3 %gather_fusion = f32[25600,8]{1,0:T(8,128)} fusion(f32[8,128]{0,1:T(8,128)S(1)} %get-tuple-element.562, s32[25600]{0:T(1024)S(1)} %broadcast_clamp_fusion.2), kind=kCustom, calls=%fused_computation.clone.clone.1 | custom fusion | bytes 1740800 | tf_op jit(solution)/shard_map/while/body/eval_jaxpr/gather | solution.py:40
  1865.0 13.8 all-gather.3.cloned.1.call-done
  1892.6 96.3 %all-gather.5.cloned.1.call-done = bf16[160,8192]{1,0:T(8,128)(2,1)} async-done(((bf16[160,128]{1,0:T(8,128)(2,1)}), bf16[160,8192]{1,0:T(8,128)(2,1)}) %all-gather.5.cloned.1.call-update) | async-done | bytes 2621456 | tf_op jit(solution)/shard_map/while/body/eval_jaxpr/all_gather | solution.py:77
  1992.7 41.6 %all-reduce.3.cloned.1.call-done = bf16[2,160,128]{2,1,0:T(8,128)(2,1)} async-done(((bf16[2,160,128]{2,1,0:T(8,128)(2,1)}), bf16[2,160,128]{2,1,0:T(8,128)(2,1)}) %all-reduce.3.cloned.1.call-update) | async-done | bytes 81936 | tf_op jit(solution)/shard_map/psum | solution.py:18
  (226 shorter events, 159.2 us)
Async XLA Ops:
  10.1 286.6 %all-gather.3.cloned.1.call-start = ((), (), s32[]{:S(2)}) async-start(), calls=%async_computation.1 | async-start | bytes 2662400 | tf_op jit(solution)/shard_map/while/body/eval_jaxpr/all_gather | solution.py:67
  10.1 6.3 collective-permute-start
  186.8 220.0 %all-gather.5.cloned.1.call-start = ((), (), s32[]{:S(2)}) async-start(), calls=%async_computation.2 | async-start | bytes 2662400 | tf_op jit(solution)/shard_map/while/body/eval_jaxpr/all_gather | solution.py:77
  301.8 105.1 %copy-start = (bf16[8192,128]{1,0:T(8,128)(2,1)S(1)}, bf16[8192,128]{1,0:T(8,128)(2,1)}, u32[]{:S(2)}) copy-start(bf16[8192,128]{1,0:T(8,128)(2,1)} %get-tuple-element.564) | copy-start | bytes 6291460 | tf_op jit(solution)/shard_map/while
  410.1 282.2 %all-gather.3.cloned.1.call-start = ((), (), s32[]{:S(2)}) async-start(), calls=%async_computation.1 | async-start | bytes 2662400 | tf_op jit(solution)/shard_map/while/body/eval_jaxpr/all_gather | solution.py:67
  410.9 3.3 collective-permute-start
  582.1 220.2 %all-gather.5.cloned.1.call-start = ((), (), s32[]{:S(2)}) async-start(), calls=%async_computation.2 | async-start | bytes 2662400 | tf_op jit(solution)/shard_map/while/body/eval_jaxpr/all_gather | solution.py:77
  692.3 5.2 copy-start.7
  692.3 5.2 copy-start.8
  697.4 104.9 %copy-start = (bf16[8192,128]{1,0:T(8,128)(2,1)S(1)}, bf16[8192,128]{1,0:T(8,128)(2,1)}, u32[]{:S(2)}) copy-start(bf16[8192,128]{1,0:T(8,128)(2,1)} %get-tuple-element.564) | copy-start | bytes 6291460 | tf_op jit(solution)/shard_map/while
  805.6 282.2 %all-gather.3.cloned.1.call-start = ((), (), s32[]{:S(2)}) async-start(), calls=%async_computation.1 | async-start | bytes 2662400 | tf_op jit(solution)/shard_map/while/body/eval_jaxpr/all_gather | solution.py:67
  806.4 3.3 collective-permute-start
  977.6 220.2 %all-gather.5.cloned.1.call-start = ((), (), s32[]{:S(2)}) async-start(), calls=%async_computation.2 | async-start | bytes 2662400 | tf_op jit(solution)/shard_map/while/body/eval_jaxpr/all_gather | solution.py:77
  1087.8 5.2 copy-start.7
  1093.0 104.9 %copy-start = (bf16[8192,128]{1,0:T(8,128)(2,1)S(1)}, bf16[8192,128]{1,0:T(8,128)(2,1)}, u32[]{:S(2)}) copy-start(bf16[8192,128]{1,0:T(8,128)(2,1)} %get-tuple-element.564) | copy-start | bytes 6291460 | tf_op jit(solution)/shard_map/while
  1201.1 282.2 %all-gather.3.cloned.1.call-start = ((), (), s32[]{:S(2)}) async-start(), calls=%async_computation.1 | async-start | bytes 2662400 | tf_op jit(solution)/shard_map/while/body/eval_jaxpr/all_gather | solution.py:67
  1201.9 3.3 collective-permute-start
  1373.1 220.2 %all-gather.5.cloned.1.call-start = ((), (), s32[]{:S(2)}) async-start(), calls=%async_computation.2 | async-start | bytes 2662400 | tf_op jit(solution)/shard_map/while/body/eval_jaxpr/all_gather | solution.py:77
  1488.4 104.9 %copy-start = (bf16[8192,128]{1,0:T(8,128)(2,1)S(1)}, bf16[8192,128]{1,0:T(8,128)(2,1)}, u32[]{:S(2)}) copy-start(bf16[8192,128]{1,0:T(8,128)(2,1)} %get-tuple-element.564) | copy-start | bytes 6291460 | tf_op jit(solution)/shard_map/while
  1596.6 282.2 %all-gather.3.cloned.1.call-start = ((), (), s32[]{:S(2)}) async-start(), calls=%async_computation.1 | async-start | bytes 2662400 | tf_op jit(solution)/shard_map/while/body/eval_jaxpr/all_gather | solution.py:67
  1597.4 3.3 collective-permute-start
  1768.6 220.2 %all-gather.5.cloned.1.call-start = ((), (), s32[]{:S(2)}) async-start(), calls=%async_computation.2 | async-start | bytes 2662400 | tf_op jit(solution)/shard_map/while/body/eval_jaxpr/all_gather | solution.py:77
  1883.9 104.9 %copy-start = (bf16[8192,128]{1,0:T(8,128)(2,1)S(1)}, bf16[8192,128]{1,0:T(8,128)(2,1)}, u32[]{:S(2)}) copy-start(bf16[8192,128]{1,0:T(8,128)(2,1)} %get-tuple-element.564) | copy-start | bytes 6291460 | tf_op jit(solution)/shard_map/while
  1992.1 42.3 %all-reduce.3.cloned.1.call-start = ((), (), s32[]{:S(2)}) async-start(), calls=%async_computation | async-start | bytes 163840 | tf_op jit(solution)/shard_map/psum | solution.py:18
  (37 other events, 169.1 us)
Sparse Core Ops, SparseCore 0:
  187.0 109.6 all-gather.2
  310.6 96.2 all-gather.4
  582.2 110.0 all-gather.2
  706.2 96.1 all-gather.4
  977.7 110.0 all-gather.2
  1101.7 96.1 all-gather.4
  1373.2 110.0 all-gather.2
  1497.2 96.1 all-gather.4
  1768.7 110.0 all-gather.2
  1892.7 96.1 all-gather.4
Sparse Core Ops, SparseCore 1:
  1995.2 39.2 all-reduce.2
where the time goes:
time: 2050 us; the launch traced here: 2040 us
  blocking collectives  832 us (41%)
  waiting for transfers between devices  592 us (29%)
  local copies, waits for them, and re-layouts  502 us (24%)
  matrix products  61.6 us (3%)
  other arithmetic  26.4 us (1%)
    psum x5, blocking collectives, layer_step(): squares = lax.psum(jnp.sum(widened * widened, axis=1), 'fsdp')  832 us
    all_gather x5, waiting for transfers between devices, layer_step(): lax.all_gather(gated, 'fsdp', axis=1, tiled=True)  482 us
    gather x10, local copies, waits for them, and re-layouts, long_mix(): kernels[:, lag_index]  470 us
    all_gather x5, waiting for transfers between devices, layer_step(): lax.all_gather(normalized, 'fsdp', axis=1, tiled=True)  68.8 us
    psum x1, waiting for transfers between devices, spread(): return lax.psum(jnp.where(mine, value, jnp.zeros_like(value)), axis)  41.6 us
  transfers between devices with their start and end apart: 16, of which 11 were waited for; matrix products, arithmetic and copies ran while one was open for 24% of the time, Pallas kernels for 0%

commit v1 on v0

--- a/solution.py
+++ b/solution.py
@@ -58,7 +58,7 @@
 
     def layer_step(activation):
         widened = activation.astype(jnp.float32)
-        squares = lax.psum(jnp.sum(widened * widened, axis=1), "fsdp")
+        squares = jnp.sum(lax.all_gather(jnp.sum(widened * widened, axis=1), "fsdp"), axis=0)
         inverse_rms = lax.rsqrt(squares / D + 1e-06)[:, None]
         normalized = (widened * inverse_rms * gain.astype(jnp.float32)).astype(jnp.bfloat16)
         weight_rows = in_weights

time: 2050 us -> 2970 us (1.45)
  blocking collectives: 832 us -> 1620 us
  waiting for transfers between devices: 592 us -> 721 us
    while x0 -> x5, blocking collectives: none -> 1620 us
    psum x5 -> x0, blocking collectives: 832 us -> none  [layer_step(): squares = lax.psum(jnp.sum(widened * widened, axis=1), 'fsdp')]
    all_gather x5, waiting for transfers between devices: 68.8 us -> 200 us  [layer_step(): lax.all_gather(normalized, 'fsdp', axis=1, tiled=True)]
  transfers between devices with their start and end apart: 16 -> 16, of which waited for: 11 -> 11; matrix products, arithmetic and copies ran while one was open for 24% -> 17% of each run, Pallas kernels for 0% -> 0%
where the time goes in v1:
time: 2970 us; the launch traced here: 2960 us
  blocking collectives  1620 us (55%)
  waiting for transfers between devices  721 us (24%)
  local copies, waits for them, and re-layouts  507 us (17%)
  matrix products  61.6 us (2%)
    while x5, blocking collectives  1620 us
    all_gather x5, waiting for transfers between devices, layer_step(): lax.all_gather(gated, 'fsdp', axis=1, tiled=True)  478 us
    gather x10, local copies, waits for them, and re-layouts, long_mix(): kernels[:, lag_index]  467 us
    all_gather x5, waiting for transfers between devices, layer_step(): lax.all_gather(normalized, 'fsdp', axis=1, tiled=True)  200 us
  transfers between devices with their start and end apart: 16, of which 11 were waited for; matrix products, arithmetic and copies ran while one was open for 17% of the time, Pallas kernels for 0%

profile of v1, /device:TPU:1, one launch (start us, length us, event | category | flops | bytes accessed | tf_op | source)
XLA Modules:
  0.0 2962.9 jit_solution(7122703678829182881)
XLA Ops:
  10.1 2901.7 %while.18 = (s32[]{:T(128)}, bf16[160,128]{1,0:T(8,128)(2,1)}, bf16[2,160,128]{2,1,0:T(8,128)(2,1)}, pred[]{:T(512)}, s32[]{:T(128)}, /*index=5*/s32[2,160]{1,0:...) while((s32[]{:T(128)}, bf16[160,128]{1,0:T(8,128)(2,1)}, ...), condition=%wide.region_3.4_spmd.clone, body=%wide.region_0.3_spmd.clone.sunk | while | flops 1404323968 | bytes 46739644 | solution.py:104
  19.8 325.7 %all-reduce.4 = f32[10240]{0:T(1024)S(1)} all-reduce(f32[10240]{0:T(1024)S(1)} %dynamic-update-slice.9), channel_id=2, replica_groups=mesh['pipe'=4,'fsdp'=64] {'fsdp'}, use_global_device_ids=true, to_apply=%add.1 | all-reduce | flops 10240 | bytes 81920 | tf_op jit(solution)/shard_map/while
  346.6 84.6 %gather_fusion = f32[25600,8]{1,0:T(8,128)} fusion(f32[8,128]{0,1:T(8,128)S(1)} %get-tuple-element.570, s32[25600]{0:T(1024)S(1)} %broadcast_clamp_fusion.2), kind=kCustom, calls=%fused_computation.clone.clone.1 | custom fusion | bytes 1740800 | tf_op jit(solution)/shard_map/while/body/eval_jaxpr/gather | solution.py:40
  431.3 8.7 copy.30
  442.1 39.4 %all-gather.4.cloned.1.call-done = bf16[160,8192]{1,0:T(8,128)(2,1)} async-done(((bf16[160,128]{1,0:T(8,128)(2,1)}), bf16[160,8192]{1,0:T(8,128)(2,1)}) %all-gather.4.cloned.1.call-update) | async-done | bytes 2621456 | tf_op jit(solution)/shard_map/while/body/eval_jaxpr/all_gather | solution.py:67
  495.3 95.7 %all-gather.6.cloned.1.call-done = bf16[160,8192]{1,0:T(8,128)(2,1)} async-done(((bf16[160,128]{1,0:T(8,128)(2,1)}), bf16[160,8192]{1,0:T(8,128)(2,1)}) %all-gather.6.cloned.1.call-update) | async-done | bytes 2621456 | tf_op jit(solution)/shard_map/while/body/eval_jaxpr/all_gather | solution.py:77
  601.5 322.5 %all-reduce.4 = f32[10240]{0:T(1024)S(1)} all-reduce(f32[10240]{0:T(1024)S(1)} %dynamic-update-slice.9), channel_id=2, replica_groups=mesh['pipe'=4,'fsdp'=64] {'fsdp'}, use_global_device_ids=true, to_apply=%add.1 | all-reduce | flops 10240 | bytes 81920 | tf_op jit(solution)/shard_map/while
  925.2 84.6 %gather_fusion = f32[25600,8]{1,0:T(8,128)} fusion(f32[8,128]{0,1:T(8,128)S(1)} %get-tuple-element.570, s32[25600]{0:T(1024)S(1)} %broadcast_clamp_fusion.2), kind=kCustom, calls=%fused_computation.clone.clone.1 | custom fusion | bytes 1740800 | tf_op jit(solution)/shard_map/while/body/eval_jaxpr/gather | solution.py:40
  1020.6 40.3 %all-gather.4.cloned.1.call-done = bf16[160,8192]{1,0:T(8,128)(2,1)} async-done(((bf16[160,128]{1,0:T(8,128)(2,1)}), bf16[160,8192]{1,0:T(8,128)(2,1)}) %all-gather.4.cloned.1.call-update) | async-done | bytes 2621456 | tf_op jit(solution)/shard_map/while/body/eval_jaxpr/all_gather | solution.py:67
  1074.6 95.7 %all-gather.6.cloned.1.call-done = bf16[160,8192]{1,0:T(8,128)(2,1)} async-done(((bf16[160,128]{1,0:T(8,128)(2,1)}), bf16[160,8192]{1,0:T(8,128)(2,1)}) %all-gather.6.cloned.1.call-update) | async-done | bytes 2621456 | tf_op jit(solution)/shard_map/while/body/eval_jaxpr/all_gather | solution.py:77
  1180.9 322.5 %all-reduce.4 = f32[10240]{0:T(1024)S(1)} all-reduce(f32[10240]{0:T(1024)S(1)} %dynamic-update-slice.9), channel_id=2, replica_groups=mesh['pipe'=4,'fsdp'=64] {'fsdp'}, use_global_device_ids=true, to_apply=%add.1 | all-reduce | flops 10240 | bytes 81920 | tf_op jit(solution)/shard_map/while
  1504.6 84.6 %gather_fusion = f32[25600,8]{1,0:T(8,128)} fusion(f32[8,128]{0,1:T(8,128)S(1)} %get-tuple-element.570, s32[25600]{0:T(1024)S(1)} %broadcast_clamp_fusion.2), kind=kCustom, calls=%fused_computation.clone.clone.1 | custom fusion | bytes 1740800 | tf_op jit(solution)/shard_map/while/body/eval_jaxpr/gather | solution.py:40
  1589.2 8.7 copy.30
  1600.0 40.3 %all-gather.4.cloned.1.call-done = bf16[160,8192]{1,0:T(8,128)(2,1)} async-done(((bf16[160,128]{1,0:T(8,128)(2,1)}), bf16[160,8192]{1,0:T(8,128)(2,1)}) %all-gather.4.cloned.1.call-update) | async-done | bytes 2621456 | tf_op jit(solution)/shard_map/while/body/eval_jaxpr/all_gather | solution.py:67
  1654.1 95.7 %all-gather.6.cloned.1.call-done = bf16[160,8192]{1,0:T(8,128)(2,1)} async-done(((bf16[160,128]{1,0:T(8,128)(2,1)}), bf16[160,8192]{1,0:T(8,128)(2,1)}) %all-gather.6.cloned.1.call-update) | async-done | bytes 2621456 | tf_op jit(solution)/shard_map/while/body/eval_jaxpr/all_gather | solution.py:77
  1760.4 322.5 %all-reduce.4 = f32[10240]{0:T(1024)S(1)} all-reduce(f32[10240]{0:T(1024)S(1)} %dynamic-update-slice.9), channel_id=2, replica_groups=mesh['pipe'=4,'fsdp'=64] {'fsdp'}, use_global_device_ids=true, to_apply=%add.1 | all-reduce | flops 10240 | bytes 81920 | tf_op jit(solution)/shard_map/while
  2084.0 84.6 %gather_fusion = f32[25600,8]{1,0:T(8,128)} fusion(f32[8,128]{0,1:T(8,128)S(1)} %get-tuple-element.570, s32[25600]{0:T(1024)S(1)} %broadcast_clamp_fusion.2), kind=kCustom, calls=%fused_computation.clone.clone.1 | custom fusion | bytes 1740800 | tf_op jit(solution)/shard_map/while/body/eval_jaxpr/gather | solution.py:40
  2179.4 40.3 %all-gather.4.cloned.1.call-done = bf16[160,8192]{1,0:T(8,128)(2,1)} async-done(((bf16[160,128]{1,0:T(8,128)(2,1)}), bf16[160,8192]{1,0:T(8,128)(2,1)}) %all-gather.4.cloned.1.call-update) | async-done | bytes 2621456 | tf_op jit(solution)/shard_map/while/body/eval_jaxpr/all_gather | solution.py:67
  2233.5 95.6 %all-gather.6.cloned.1.call-done = bf16[160,8192]{1,0:T(8,128)(2,1)} async-done(((bf16[160,128]{1,0:T(8,128)(2,1)}), bf16[160,8192]{1,0:T(8,128)(2,1)}) %all-gather.6.cloned.1.call-update) | async-done | bytes 2621456 | tf_op jit(solution)/shard_map/while/body/eval_jaxpr/all_gather | solution.py:77
  2339.8 322.5 %all-reduce.4 = f32[10240]{0:T(1024)S(1)} all-reduce(f32[10240]{0:T(1024)S(1)} %dynamic-update-slice.9), channel_id=2, replica_groups=mesh['pipe'=4,'fsdp'=64] {'fsdp'}, use_global_device_ids=true, to_apply=%add.1 | all-reduce | flops 10240 | bytes 81920 | tf_op jit(solution)/shard_map/while
  2663.5 84.6 %gather_fusion = f32[25600,8]{1,0:T(8,128)} fusion(f32[8,128]{0,1:T(8,128)S(1)} %get-tuple-element.570, s32[25600]{0:T(1024)S(1)} %broadcast_clamp_fusion.2), kind=kCustom, calls=%fused_computation.clone.clone.1 | custom fusion | bytes 1740800 | tf_op jit(solution)/shard_map/while/body/eval_jaxpr/gather | solution.py:40
  2758.9 40.3 %all-gather.4.cloned.1.call-done = bf16[160,8192]{1,0:T(8,128)(2,1)} async-done(((bf16[160,128]{1,0:T(8,128)(2,1)}), bf16[160,8192]{1,0:T(8,128)(2,1)}) %all-gather.4.cloned.1.call-update) | async-done | bytes 2621456 | tf_op jit(solution)/shard_map/while/body/eval_jaxpr/all_gather | solution.py:67
  2813.0 95.7 %all-gather.6.cloned.1.call-done = bf16[160,8192]{1,0:T(8,128)(2,1)} async-done(((bf16[160,128]{1,0:T(8,128)(2,1)}), bf16[160,8192]{1,0:T(8,128)(2,1)}) %all-gather.6.cloned.1.call-update) | async-done | bytes 2621456 | tf_op jit(solution)/shard_map/while/body/eval_jaxpr/all_gather | solution.py:77
  2912.5 41.6 %all-reduce.7.cloned.1.call-done = bf16[2,160,128]{2,1,0:T(8,128)(2,1)} async-done(((bf16[2,160,128]{2,1,0:T(8,128)(2,1)}), bf16[2,160,128]{2,1,0:T(8,128)(2,1)}) %all-reduce.7.cloned.1.call-update) | async-done | bytes 81936 | tf_op jit(solution)/shard_map/psum | solution.py:18
  (251 shorter events, 167.3 us)
Async XLA Ops:
  10.1 471.3 %all-gather.4.cloned.1.call-start = ((), (), s32[]{:S(2)}) async-start(), calls=%async_computation.1 | async-start | bytes 2662400 | tf_op jit(solution)/shard_map/while/body/eval_jaxpr/all_gather | solution.py:67
  10.1 8.1 collective-permute-start
  346.4 244.5 %all-gather.6.cloned.1.call-start = ((), (), s32[]{:S(2)}) async-start(), calls=%async_computation.2 | async-start | bytes 2662400 | tf_op jit(solution)/shard_map/while/body/eval_jaxpr/all_gather | solution.py:77
  481.4 5.2 copy-start.7
  486.6 104.3 %copy-start = (bf16[8192,128]{1,0:T(8,128)(2,1)S(1)}, bf16[8192,128]{1,0:T(8,128)(2,1)}, u32[]{:S(2)}) copy-start(bf16[8192,128]{1,0:T(8,128)(2,1)} %get-tuple-element.572) | copy-start | bytes 6291460 | tf_op jit(solution)/shard_map/while
  594.1 466.7 %all-gather.4.cloned.1.call-start = ((), (), s32[]{:S(2)}) async-start(), calls=%async_computation.1 | async-start | bytes 2662400 | tf_op jit(solution)/shard_map/while/body/eval_jaxpr/all_gather | solution.py:67
  594.9 5.1 collective-permute-start
  924.9 245.4 %all-gather.6.cloned.1.call-start = ((), (), s32[]{:S(2)}) async-start(), calls=%async_computation.2 | async-start | bytes 2662400 | tf_op jit(solution)/shard_map/while/body/eval_jaxpr/all_gather | solution.py:77
  1066.0 104.3 %copy-start = (bf16[8192,128]{1,0:T(8,128)(2,1)S(1)}, bf16[8192,128]{1,0:T(8,128)(2,1)}, u32[]{:S(2)}) copy-start(bf16[8192,128]{1,0:T(8,128)(2,1)} %get-tuple-element.572) | copy-start | bytes 6291460 | tf_op jit(solution)/shard_map/while
  1173.5 466.8 %all-gather.4.cloned.1.call-start = ((), (), s32[]{:S(2)}) async-start(), calls=%async_computation.1 | async-start | bytes 2662400 | tf_op jit(solution)/shard_map/while/body/eval_jaxpr/all_gather | solution.py:67
  1174.3 5.1 collective-permute-start
  1504.3 245.4 %all-gather.6.cloned.1.call-start = ((), (), s32[]{:S(2)}) async-start(), calls=%async_computation.2 | async-start | bytes 2662400 | tf_op jit(solution)/shard_map/while/body/eval_jaxpr/all_gather | solution.py:77
  1645.4 104.3 %copy-start = (bf16[8192,128]{1,0:T(8,128)(2,1)S(1)}, bf16[8192,128]{1,0:T(8,128)(2,1)}, u32[]{:S(2)}) copy-start(bf16[8192,128]{1,0:T(8,128)(2,1)} %get-tuple-element.572) | copy-start | bytes 6291460 | tf_op jit(solution)/shard_map/while
  1753.0 466.7 %all-gather.4.cloned.1.call-start = ((), (), s32[]{:S(2)}) async-start(), calls=%async_computation.1 | async-start | bytes 2662400 | tf_op jit(solution)/shard_map/while/body/eval_jaxpr/all_gather | solution.py:67
  1753.8 5.1 collective-permute-start
  2083.8 245.4 %all-gather.6.cloned.1.call-start = ((), (), s32[]{:S(2)}) async-start(), calls=%async_computation.2 | async-start | bytes 2662400 | tf_op jit(solution)/shard_map/while/body/eval_jaxpr/all_gather | solution.py:77
  2219.7 5.2 copy-start.7
  2219.7 5.2 copy-start.8
  2224.8 104.3 %copy-start = (bf16[8192,128]{1,0:T(8,128)(2,1)S(1)}, bf16[8192,128]{1,0:T(8,128)(2,1)}, u32[]{:S(2)}) copy-start(bf16[8192,128]{1,0:T(8,128)(2,1)} %get-tuple-element.572) | copy-start | bytes 6291460 | tf_op jit(solution)/shard_map/while
  2332.4 466.8 %all-gather.4.cloned.1.call-start = ((), (), s32[]{:S(2)}) async-start(), calls=%async_computation.1 | async-start | bytes 2662400 | tf_op jit(solution)/shard_map/while/body/eval_jaxpr/all_gather | solution.py:67
  2333.2 5.1 collective-permute-start
  2663.2 245.4 %all-gather.6.cloned.1.call-start = ((), (), s32[]{:S(2)}) async-start(), calls=%async_computation.2 | async-start | bytes 2662400 | tf_op jit(solution)/shard_map/while/body/eval_jaxpr/all_gather | solution.py:77
  2804.3 104.3 %copy-start = (bf16[8192,128]{1,0:T(8,128)(2,1)S(1)}, bf16[8192,128]{1,0:T(8,128)(2,1)}, u32[]{:S(2)}) copy-start(bf16[8192,128]{1,0:T(8,128)(2,1)} %get-tuple-element.572) | copy-start | bytes 6291460 | tf_op jit(solution)/shard_map/while
  2911.8 42.3 %all-reduce.7.cloned.1.call-start = ((), (), s32[]{:S(2)}) async-start(), calls=%async_computation | async-start | bytes 163840 | tf_op jit(solution)/shard_map/psum | solution.py:18
  (37 other events, 169.2 us)
Sparse Core Ops, SparseCore 0:
  346.5 134.8 all-gather.3
  495.4 95.4 all-gather.5
  925.0 135.7 all-gather.3
  1074.7 95.5 all-gather.5
  1504.5 135.7 all-gather.3
  1654.2 95.5 all-gather.5
  2083.9 135.7 all-gather.3
  2233.6 95.4 all-gather.5
  2663.3 135.7 all-gather.3
  2813.1 95.5 all-gather.5
Sparse Core Ops, SparseCore 1:
  2914.9 39.2 all-reduce.6
